TPU v7x, 32 devices: a whole 2x2x4 slice. The times are simulated.
32 devices in a mesh: dom: 8 (over z, x), rep: 4 (over y, core).
Axes of the slice: x: 2, y: 2, z: 4, core: 2. Of those that a mesh axis runs over, the one named last changes fastest.
Arguments:
- features: bfloat16 [131072, 100], P(('dom', 'rep')), may hold values from -6 to 6
- labels: int32 [65536], P(('dom', 'rep')), may hold values from 0 to 46
- seed_rows: int32 [65536], P(('dom', 'rep')), may hold values from 0 to 4095
- seed_mask: int32 [65536], P(('dom', 'rep')), may hold values from 0 to 1
- send_rows: int32 [1024, 16], P(('dom', 'rep')), may hold values from 0 to 4095
- neighbors_one: int32 [131072, 15], P(('dom', 'rep')), may hold values from 0 to 4607, as said below
- neighbors_two: int32 [131072, 10], P(('dom', 'rep')), may hold values from 0 to 4607, as said below
- neighbors_three: int32 [131072, 5], P(('dom', 'rep')), may hold values from 0 to 4607, as said below
- weight_one: float32 [200, 256], replicated, may hold values from -0.625 to 0.625
- weight_two: float32 [512, 256], replicated, may hold values from -6 to 6
- weight_three: float32 [512, 47], replicated, may hold values from -12 to 12
- left_one: float32 [200, 200], replicated, as said below
- right_one: float32 [256, 256], replicated, as said below
- left_two: float32 [512, 512], replicated, as said below
- right_two: float32 [256, 256], replicated, as said below
- left_three: float32 [512, 512], replicated, as said below
- right_three: float32 [47, 47], replicated, as said below
- first_one: float32 [200, 256], replicated
- first_two: float32 [512, 256], replicated
- first_three: float32 [512, 47], replicated
- second_one: float32 [200, 256], replicated
- second_two: float32 [512, 256], replicated, may hold values from 1.5258789e-12 to 6.1035157e-12
- second_three: float32 [512, 47], replicated, may hold values from 1.5258789e-12 to 6.1035157e-12
- bias_all: float32 [559], replicated, may hold values from -0.6 to 0.6
- bias_first: float32 [559], replicated
- bias_second: float32 [559], replicated, may hold values from 1.5258789e-10 to 6.1035155e-10
Outputs:
- new_weight_one: float32 [200, 256], replicated
- new_first_one: float32 [200, 256], replicated
- new_second_one: float32 [200, 256], replicated
- new_weight_two: float32 [512, 256], replicated
- new_first_two: float32 [512, 256], replicated
- new_second_two: float32 [512, 256], replicated
- new_weight_three: float32 [512, 47], replicated
- new_first_three: float32 [512, 47], replicated
- new_second_three: float32 [512, 47], replicated
- new_bias: float32 [559], replicated
- new_bias_first: float32 [559], replicated
- new_bias_second: float32 [559], replicated
- loss_sum: float32 [], replicated
- seed_total: float32 [], replicated
Inputs may be any that keep to these rules, and one draw needn't show every extreme that they name: `neighbors_one`: entries below 4096 name the part's own nodes, the others its halo rows; column 0 of a part's lists names every halo row of that part at least once. `neighbors_two`: as for neighbors_one. `neighbors_three`: as for neighbors_one. `left_one`: Orthogonal. `right_one`: Orthogonal. `left_two`: Orthogonal. `right_two`: Orthogonal. `left_three`: Orthogonal. `right_three`: Orthogonal.
All inputs are finite; a program needn't handle non-finite values.
Results may differ from a plain program's by a relative error of at most 0.0085.
Values may be sent and summed in bfloat16 or wider, within the bound.
A program may use at most 256 MiB of HBM per device.

v0:
```python
import jax
import jax.numpy as jnp
from jax import lax
from jax.sharding import PartitionSpec as P

STEP = 10


beta_one = 0.9
beta_two = 0.999
epsilon = 1e-08
step_rates = (0.05, 0.5, 1.0)
bias_rate = 0.05
weight_decay = 0.01


def product(left, right):
    return jnp.dot(left, right, precision=lax.Precision.HIGHEST, preferred_element_type=jnp.float32)


def activate(preact):
    active = jax.nn.silu(preact)
    return active * lax.rsqrt(jnp.sum(active * active, axis=-1, keepdims=True) + 1e-06)


def send_halo(blocks):
    return lax.all_to_all(blocks, ("dom", "rep"), split_axis=0, concat_axis=0, tiled=True)


def return_halo(blocks):
    return lax.all_to_all(blocks, ("dom", "rep"), split_axis=0, concat_axis=0, tiled=True)


def layer_forward(states, weight, bias_part, neighbors, send_rows, last):
    rounded = states.astype(jnp.bfloat16)
    in_width = rounded.shape[1]
    local_rows = rounded.shape[0]
    received = send_halo(rounded[send_rows])
    lookup = jnp.concatenate([rounded, received.reshape(-1, in_width)], axis=0)
    fanout = neighbors.shape[1]
    picked = lookup[neighbors.reshape(-1)].reshape(local_rows, fanout, in_width)
    summed = jnp.sum(picked.astype(jnp.float32), axis=1)
    mean = (summed / fanout).astype(jnp.bfloat16)
    weight_low = weight.astype(jnp.bfloat16)
    preact = jnp.dot(rounded, weight_low[:in_width], preferred_element_type=jnp.float32)
    preact = (
        preact
        + jnp.dot(mean, weight_low[in_width:], preferred_element_type=jnp.float32)
        + bias_part
    )
    output = preact if last else activate(preact)
    return ((rounded, lookup, mean, preact), output)


def layer_backward(grad_out, saved, weight, neighbors, send_rows, last, first):
    rounded, lookup, mean, preact = saved
    if last:
        grad_pre = grad_out
    else:
        pullback = jax.vjp(activate, preact)[1]
        grad_pre = pullback(grad_out)[0]
    grad_low = grad_pre.astype(jnp.bfloat16)
    grad_bias = jnp.sum(grad_low.astype(jnp.float32), axis=0)
    over_rows = (((0,), (0,)), ((), ()))
    grad_weight = jnp.concatenate(
        [
            lax.dot_general(rounded, grad_low, over_rows, preferred_element_type=jnp.float32),
            lax.dot_general(mean, grad_low, over_rows, preferred_element_type=jnp.float32),
        ],
        axis=0,
    )
    if first:
        return (grad_weight, grad_bias, None)
    in_width = rounded.shape[1]
    local_rows = rounded.shape[0]
    fanout = neighbors.shape[1]
    weight_low = weight.astype(jnp.bfloat16)
    over_cols = (((1,), (1,)), ((), ()))
    grad_self = lax.dot_general(
        grad_low, weight_low[:in_width], over_cols, preferred_element_type=jnp.float32
    )
    grad_mean = (
        lax.dot_general(
            grad_low, weight_low[in_width:], over_cols, preferred_element_type=jnp.float32
        )
        / fanout
    )
    spread = jnp.broadcast_to(grad_mean[:, None, :], (local_rows, fanout, in_width)).reshape(
        -1, in_width
    )
    grad_lookup = (
        jnp.zeros((lookup.shape[0], in_width), jnp.float32).at[neighbors.reshape(-1)].add(spread)
    )
    halo_grad = grad_lookup[local_rows:].astype(jnp.bfloat16).reshape(send_rows.shape + (in_width,))
    returned = return_halo(halo_grad)
    grad_state = grad_self + grad_lookup[:local_rows]
    grad_state = grad_state.at[send_rows.reshape(-1)].add(
        returned.reshape(-1, in_width).astype(jnp.float32)
    )
    return (grad_weight, grad_bias, grad_state)


def rotate_adam(weight, grad, first, second, left_basis, right_basis, rate):
    turned = product(product(left_basis.T, grad), right_basis)
    first = beta_one * first + (1.0 - beta_one) * turned
    second = beta_two * second + (1.0 - beta_two) * turned * turned
    update = first / (1.0 - beta_one**STEP) / (jnp.sqrt(second / (1.0 - beta_two**STEP)) + epsilon)
    return (weight - rate * product(product(left_basis, update), right_basis.T), first, second)


def on_device(
    features,
    labels,
    seed_rows,
    seed_mask,
    send_rows,
    neighbors_one,
    neighbors_two,
    neighbors_three,
    weight_one,
    weight_two,
    weight_three,
    left_one,
    right_one,
    left_two,
    right_two,
    left_three,
    right_three,
    first_one,
    first_two,
    first_three,
    second_one,
    second_two,
    second_three,
    bias_all,
    bias_first,
    bias_second,
):
    hidden_width = weight_one.shape[1]
    weights = (weight_one, weight_two, weight_three)
    biases = (
        bias_all[:hidden_width],
        bias_all[hidden_width : 2 * hidden_width],
        bias_all[2 * hidden_width :],
    )
    neighbor_list = (neighbors_one, neighbors_two, neighbors_three)
    inputs = []
    kept = []
    states = features
    for layer in range(3):
        inputs.append(states)
        saved, states = layer_forward(
            states, weights[layer], biases[layer], neighbor_list[layer], send_rows, layer == 2
        )
        kept.append(saved)
    picked_rows = states[seed_rows]
    normer = jax.scipy.special.logsumexp(picked_rows, axis=-1)
    classes = lax.broadcasted_iota(jnp.int32, picked_rows.shape, 1)
    onehot = (classes == labels[:, None]).astype(jnp.float32)
    seed_float = seed_mask.astype(jnp.float32)
    local_loss = jnp.sum((normer - jnp.sum(picked_rows * onehot, axis=-1)) * seed_float)
    loss_sum, seed_total = lax.psum((local_loss, jnp.sum(seed_float)), ("dom", "rep"))
    grad_rows = (jnp.exp(picked_rows - normer[:, None]) - onehot) * (seed_float / seed_total)[
        :, None
    ]
    grad_out = jnp.zeros(states.shape, jnp.float32).at[seed_rows].add(grad_rows)
    grad_weights = [None, None, None]
    grad_biases = [None, None, None]
    for layer in (2, 1, 0):
        saved = kept[layer]
        if layer < 2:
            saved = layer_forward(
                inputs[layer], weights[layer], biases[layer], neighbor_list[layer], send_rows, False
            )[0]
        grad_weights[layer], grad_biases[layer], grad_out = layer_backward(
            grad_out, saved, weights[layer], neighbor_list[layer], send_rows, layer == 2, layer == 0
        )
    grad_bias_all = jnp.concatenate(grad_biases, axis=0)
    summed = lax.psum(
        (grad_weights[0], grad_weights[1], grad_weights[2], grad_bias_all), ("dom", "rep")
    )
    out_one = rotate_adam(
        weight_one, summed[0], first_one, second_one, left_one, right_one, step_rates[0]
    )
    out_two = rotate_adam(
        weight_two, summed[1], first_two, second_two, left_two, right_two, step_rates[1]
    )
    out_three = rotate_adam(
        weight_three, summed[2], first_three, second_three, left_three, right_three, step_rates[2]
    )
    bias_m = beta_one * bias_first + (1.0 - beta_one) * summed[3]
    bias_v = beta_two * bias_second + (1.0 - beta_two) * summed[3] * summed[3]
    bias_update = (
        bias_m / (1.0 - beta_one**STEP) / (jnp.sqrt(bias_v / (1.0 - beta_two**STEP)) + epsilon)
    )
    new_bias = bias_all - bias_rate * (bias_update + weight_decay * bias_all)
    return (
        out_one[0],
        out_one[1],
        out_one[2],
        out_two[0],
        out_two[1],
        out_two[2],
        out_three[0],
        out_three[1],
        out_three[2],
        new_bias,
        bias_m,
        bias_v,
        loss_sum,
        seed_total,
    )


def solution(mesh):
    placed = (
        P(("dom", "rep"), None),
        P(("dom", "rep")),
        P(("dom", "rep")),
        P(("dom", "rep")),
        P(("dom", "rep"), None),
        P(("dom", "rep"), None),
        P(("dom", "rep"), None),
        P(("dom", "rep"), None),
        P(),
        P(),
        P(),
        P(),
        P(),
        P(),
        P(),
        P(),
        P(),
        P(),
        P(),
        P(),
        P(),
        P(),
        P(),
        P(),
        P(),
        P(),
    )
    return jax.shard_map(
        on_device,
        mesh=mesh,
        in_specs=placed,
        out_specs=(P(), P(), P(), P(), P(), P(), P(), P(), P(), P(), P(), P(), P(), P()),
        check_vma=False,
    )
```

profile of v0, /device:TPU:0, one launch (start us, length us, event | category | flops | bytes accessed | tf_op | source)
XLA Modules:
  0.0 1502.1 jit_solution(2765747441795827087)
XLA Ops:
  9.8 1.9 gather_fusion
  11.8 7.4 all-to-all-start
  25.0 2.0 copy.80
  27.0 3.3 reshape.242
  31.3 2.0 copy.81
  33.3 3.5 reshape.244
  37.7 2.9 copy.82
  40.5 3.1 reshape.246
  44.4 3.5 fusion.67
  49.6 232.8 %gather_fusion.1 = bf16[61440,100]{1,0:T(8,128)(2,1)} fusion(bf16[4608,100]{1,0:T(8,128)(2,1)S(1)} %pad_maximum_fusion.2, s32[61440]{0:T(1024)} %broadcast_clamp_fusion), kind=kCustom, calls=%fused_computation.1 | custom fusion | bytes 24821760 | tf_op jit(solution)/shard_map/gather | solution.py:41
  282.4 26.0 %reshape.252 = f32[4096,15,100]{2,1,0:T(8,128)} reshape(bf16[61440,100]{1,0:T(8,128)(2,1)} %gather_fusion.1) | data formatting | bytes 36864000 | tf_op jit(solution)/shard_map/convert_element_type | solution.py:42
  308.5 24.1 %reduce_sum.121 = f32[4096,100]{1,0:T(8,128)S(1)} reduce(f32[4096,15,100]{2,1,0:T(8,128)} %reshape.252, f32[]{:T(128)} %constant.21.clone.1), dimensions={1}, to_apply=%region_0.0 | reduce | flops 5734400 | bytes 26214404 | tf_op jit(solution)/shard_map/reduce_sum | solution.py:42
  332.6 4.6 multiply_reduce_fusion.3
  337.2 1.9 copy-done.5
  340.3 2.6 gather_fusion.2
  342.9 5.9 all-to-all-start.1
  349.4 2.7 fusion.54
  352.1 7.3 all-to-all-done.1
  359.4 1.8 pad_maximum_fusion
  361.2 173.8 %gather_fusion.3 = bf16[40960,256]{1,0:T(8,128)(2,1)} fusion(bf16[4608,256]{1,0:T(8,128)(2,1)S(1)} %pad_maximum_fusion, s32[40960]{0:T(1024)} %broadcast_clamp_fusion.1), kind=kCustom, calls=%fused_computation.3 | custom fusion | bytes 42106880 | tf_op jit(solution)/shard_map/gather | solution.py:41
  535.0 41.4 %reshape.253 = f32[4096,10,256]{2,1,0:T(8,128)} reshape(bf16[40960,256]{1,0:T(8,128)(2,1)} %gather_fusion.3) | data formatting | bytes 62914560 | tf_op jit(solution)/shard_map/convert_element_type | solution.py:42
  576.4 23.8 %reduce_sum.126 = f32[4096,256]{1,0:T(8,128)} reduce(f32[4096,10,256]{2,1,0:T(8,128)} %reshape.253, f32[]{:T(128)} %constant.21.clone.1), dimensions={1}, to_apply=%region_2.3 | reduce | flops 9437184 | bytes 46137348 | tf_op jit(solution)/shard_map/reduce_sum | solution.py:42
  600.2 5.1 multiply_reduce_fusion.2
  605.4 2.0 copy-done.7
  608.5 2.6 gather_fusion.4
  611.1 3.1 all-to-all-start.2
  615.9 8.9 all-to-all-done.2
  625.5 1.8 pad_maximum_fusion.1
  627.4 80.9 %gather_fusion.5 = bf16[20480,256]{1,0:T(8,128)(2,1)} fusion(bf16[4608,256]{1,0:T(8,128)(2,1)S(1)} %pad_maximum_fusion.1, s32[20480]{0:T(1024)S(1)} %copy-done.37), kind=kCustom, calls=%fused_computation.5 | custom fusion | bytes 21053440 | tf_op jit(solution)/shard_map/gather | solution.py:41
  708.3 21.6 %reshape.254 = f32[4096,5,256]{2,1,0:T(8,128)} reshape(bf16[20480,256]{1,0:T(8,128)(2,1)} %gather_fusion.5) | data formatting | bytes 31457280 | tf_op jit(solution)/shard_map/convert_element_type | solution.py:42
  730.0 25.8 %reduce_sum.128 = f32[4096,256]{1,0:T(8,128)} reduce(f32[4096,5,256]{2,1,0:T(8,128)} %reshape.254, f32[]{:T(128)} %constant.21.clone.1), dimensions={1}, to_apply=%region_4.5 | reduce | flops 4194304 | bytes 25165828 | tf_op jit(solution)/shard_map/reduce_sum | solution.py:42
  755.8 3.8 fusion.2
  759.6 1.8 copy.83
  761.4 7.6 gather_fusion.6
  770.6 2.3 select_reduce_fusion
  773.6 38.8 %psum.42 = f32[]{:T(128)} all-reduce(f32[]{:T(128)} %get-tuple-element.17), channel_id=1, replica_groups=mesh['dom'=8,'rep'=4] {'dom','rep'}, use_global_device_ids=true, to_apply=%region_8.9 | all-reduce | flops 1 | bytes 8 | tf_op jit(solution)/shard_map/psum | solution.py:162
  813.0 13.6 scatter_custom_fusion
  826.7 2.3 convert_reduce_fusion.2
  829.0 2.7 fusion.25
  833.0 11.2 broadcast_in_dim.20
  844.2 28.2 %reshape.325 = f32[20480,256]{1,0:T(8,128)} reshape(f32[4096,5,256]{2,1,0:T(8,128)} %broadcast_in_dim.20) | data formatting | bytes 41943040 | tf_op jit(solution)/shard_map/reshape | solution.py:88
  872.3 112.3 %scatter_custom_fusion.1 = f32[4608,256]{1,0:T(8,128)} fusion(s32[20480]{0:T(1024)} %bitcast.64, f32[20480,256]{1,0:T(8,128)} %reshape.325, f32[]{:T(128)} %constant.21.clone.1), kind=kCustom, calls=%fused_computation.50 | custom fusion | flops 5242880 | bytes 4719104 | tf_op jit(solution)/shard_map/scatter-add | solution.py:92
  984.6 1.8 slice.111
  986.4 3.9 all-to-all-start.3
  991.0 4.8 convolution_add_fusion.1
  995.8 5.1 all-to-all-done.3
  1000.9 7.2 scatter_custom_fusion.2
  1008.1 4.8 multiply_reduce_fusion.1
  1014.0 3.4 convert_reduce_fusion
  1021.2 21.2 %broadcast_in_dim.22 = f32[4096,10,256]{2,1,0:T(8,128)} broadcast(f32[4096,256]{1,0:T(8,128)S(1)} %convolution_multiply_fusion), dimensions={0,2} | broadcast | bytes 46137344 | tf_op jit(solution)/shard_map/broadcast_in_dim | solution.py:88
  1042.4 55.1 %reshape.341 = f32[40960,256]{1,0:T(8,128)} reshape(f32[4096,10,256]{2,1,0:T(8,128)} %broadcast_in_dim.22) | data formatting | bytes 83886080 | tf_op jit(solution)/shard_map/reshape | solution.py:88
  1097.6 221.1 %scatter_custom_fusion.3 = f32[4608,256]{1,0:T(8,128)} fusion(s32[40960]{0:T(1024)} %bitcast.62, f32[40960,256]{1,0:T(8,128)} %reshape.341, f32[]{:T(128)} %constant.21.clone.1), kind=kCustom, calls=%fused_computation.48 | custom fusion | flops 10485760 | bytes 4719104 | tf_op jit(solution)/shard_map/scatter-add | solution.py:92
  1318.6 1.8 slice.110
  1320.4 3.3 all-to-all-start.4
  1323.8 1.9 pad_maximum_fusion.3
  1325.6 4.9 convolution_add_fusion
  1330.6 3.7 all-to-all-done.4
  1334.3 7.6 scatter_custom_fusion.4
  1341.9 4.8 multiply_reduce_fusion
  1347.8 3.5 convert_reduce_fusion.1
  1353.7 38.9 %all-reduce = (f32[559]{0:T(1024)S(1)}, f32[]{:T(128)}) all-reduce(f32[559]{0:T(1024)S(1)} %pad_maximum_fusion.6, f32[]{:T(128)} %get-tuple-element.16), channel_id=1, replica_groups=mesh['dom'=8,'rep'=4] {'dom','rep'}, use_global_device_ids=true, to_apply=%region_22.23 | all-reduce | flops 560 | bytes 4480 | tf_op jit(solution)/shard_map/psum | solution.py:179
  1393.2 87.9 %all-reduce.4.cloned.1.call-done = (f32[200,256]{1,0:T(8,128)}, f32[512,256]{1,0:T(8,128)}, f32[512,47]{0,1:T(8,128)}) async-done(((f32[200,256]{1,0:T(8,128)}, f32[512,256]{1,0:T(8,128)}, f32[512,47]{0,1:T(8,128)}), (f32[200,256]{1,0:T(8,128)}, f32[512,256]{1,0:T(8,128)}, f32[512,47]{0,1:T(8,128)})) %all-reduce.4.cloned.1.call-update) | async-done | bytes 825360 | tf_op jit(solution)/shard_map/psum | solution.py:179
  1490.9 2.1 fusion.31
  1493.0 1.8 fusion.15
  (192 shorter events, 41.3 us)
Async XLA Ops:
  7.2 1481.6 %copy-start = (f32[512,512]{1,0:T(8,128)S(1)}, f32[512,512]{1,0:T(8,128)}, u32[]{:S(2)}) copy-start(f32[512,512]{1,0:T(8,128)} %param.39) | copy-start | bytes 3145732
  7.2 17.7 %copy-start.18 = (f32[512,256]{1,0:T(8,128)S(1)}, f32[512,256]{1,0:T(8,128)}, u32[]{:S(2)}) copy-start(f32[512,256]{1,0:T(8,128)} %param.35) | copy-start | bytes 1572868
  7.2 17.8 %copy-start.39 = (s32[4096,15]{0,1:T(8,128)S(1)}, s32[4096,15]{0,1:T(8,128)}, u32[]{:S(2)}) copy-start(s32[4096,15]{0,1:T(8,128)} %param.31) | copy-start | bytes 737284
  9.8 21.5 %copy-start.40 = (s32[4096,10]{0,1:T(8,128)S(1)}, s32[4096,10]{0,1:T(8,128)}, u32[]{:S(2)}) copy-start(s32[4096,10]{0,1:T(8,128)} %param.32) | copy-start | bytes 491524
  11.8 36.7 %all-to-all-start = ((bf16[32,16,100]{2,1,0:T(8,128)(2,1)}), bf16[32,16,100]{2,1,0:T(8,128)(2,1)}, u32[]{:S(2)}, u32[]{:S(2)}) async-start(bf16[32,16,100]{2,1,0:T(8,128)(2,1)} %bitcast), calls=%async_computation | async-start | bytes 262144 | tf_op jit(solution)/shard_map/all_to_all | solution.py:27
  25.0 324.4 %copy-start.22 = (bf16[512,256]{1,0:T(8,128)(2,1)}, bf16[512,256]{1,0:T(8,128)(2,1)S(1)}, u32[]{:S(2)}) copy-start(bf16[512,256]{1,0:T(8,128)(2,1)S(1)} %convert_element_type.94) | copy-start | bytes 786436
  33.3 11.1 copy-start.14
  36.9 11.0 copy-start.29
  40.5 7.4 copy-start.61
  43.7 4.8 copy-start.38
  308.5 24.1 %copy-start.41 = (bf16[200,256]{1,0:T(8,128)(2,1)S(1)}, bf16[200,256]{1,0:T(8,128)(2,1)}, u32[]{:S(2)}) copy-start(bf16[200,256]{1,0:T(8,128)(2,1)} %convert_element_type.89) | copy-start | bytes 307204
  332.5 4.7 copy-start.12
  337.2 5.7 copy-start.54
  337.2 5.7 copy-start.47
  339.1 9.7 copy-start.63
  340.3 11.8 copy-start.3
  342.9 16.5 %all-to-all-start.1 = ((bf16[32,16,256]{2,1,0:T(8,128)(2,1)}), bf16[32,16,256]{2,1,0:T(8,128)(2,1)}, u32[]{:S(2)}, u32[]{:S(2)}) async-start(bf16[32,16,256]{2,1,0:T(8,128)(2,1)} %bitcast.57), calls=%async_computation.1 | async-start | bytes 524288 | tf_op jit(solution)/shard_map/all_to_all | solution.py:27
  576.4 23.8 %copy-start.23 = (bf16[512,256]{1,0:T(8,128)(2,1)S(1)}, bf16[512,256]{1,0:T(8,128)(2,1)}, u32[]{:S(2)}) copy-start(bf16[512,256]{1,0:T(8,128)(2,1)} %copy-done.22) | copy-start | bytes 786436
  576.4 23.8 %copy-start.67 = (f32[256]{0:T(256)S(1)}, f32[256]{0:T(256)}, u32[]{:S(2)}) copy-start(f32[256]{0:T(256)} %get-tuple-element.41) | copy-start | bytes 3076
  607.3 6.9 copy-start.64
  607.3 6.9 copy-start.33
  608.5 16.3 %copy-start.1 = (bf16[4096,256]{1,0:T(8,128)(2,1)}, bf16[4096,256]{1,0:T(8,128)(2,1)S(1)}, u32[]{:S(2)}) copy-start(bf16[4096,256]{1,0:T(8,128)(2,1)S(1)} %multiply_convert_fusion.1) | copy-start | bytes 6291460
  611.1 16.3 %copy-start.37 = (s32[20480]{0:T(1024)S(1)}, s32[20480]{0:T(1024)}, u32[]{:S(2)}) copy-start(s32[20480]{0:T(1024)} %broadcast_clamp_fusion.2) | copy-start | bytes 245764
  611.1 13.7 all-to-all-start.2
  730.0 25.8 %copy-start.17 = (f32[4096,47]{0,1:T(8,128)S(1)}, f32[4096,47]{0,1:T(8,128)}, u32[]{:S(2)}) copy-start(f32[4096,47]{0,1:T(8,128)} %fusion.75) | copy-start | bytes 2310148
  730.0 25.8 %copy-start.68 = (f32[47]{0:T(128)S(1)}, f32[47]{0:T(128)}, u32[]{:S(2)}) copy-start(f32[47]{0:T(128)} %slice.57) | copy-start | bytes 568
  755.8 5.6 copy-start.60
  761.4 9.2 copy-start.58
  761.4 11.5 copy-start.59
  826.7 5.0 copy-start.2
  986.4 14.5 all-to-all-start.3
  1000.9 11.9 copy-start.57
  1008.1 4.8 copy-start.8
  1008.1 5.9 copy-start.10
  1008.1 5.9 copy-start.50
  1320.4 13.9 all-to-all-start.4
  1323.7 157.4 %all-reduce.4.cloned.1.call-start = ((), (), s32[]{:S(2)}) async-start(), calls=%async_computation.5 | async-start | bytes 1654784 | tf_op jit(solution)/shard_map/psum | solution.py:179
  1325.6 21.1 %copy-start.55 = (f32[4096]{0:T(1024)S(1)}, f32[4096]{0:T(1024)}, u32[]{:S(2)}) copy-start(f32[4096]{0:T(1024)} %copy-done.54) | copy-start | bytes 49156
  1341.9 4.8 copy-start.6
  1341.9 5.9 copy-start.9
  1341.9 5.9 copy-start.48
  1351.3 41.3 %copy-start.62 = (f32[559]{0:T(1024)S(1)}, f32[559]{0:T(1024)}, u32[]{:S(2)}) copy-start(f32[559]{0:T(1024)} %param.49) | copy-start | bytes 6712
  1351.3 41.3 %copy-start.65 = (f32[559]{0:T(1024)S(1)}, f32[559]{0:T(1024)}, u32[]{:S(2)}) copy-start(f32[559]{0:T(1024)} %param.50) | copy-start | bytes 6712
  1351.4 41.2 %copy-start.66 = (f32[559]{0:T(1024)S(1)}, f32[559]{0:T(1024)}, u32[]{:S(2)}) copy-start(f32[559]{0:T(1024)} %param.51) | copy-start | bytes 6712
  1351.4 129.8 %copy-start.16 = (f32[512,512]{1,0:T(8,128)S(1)}, f32[512,512]{1,0:T(8,128)}, u32[]{:S(2)}) copy-start(f32[512,512]{1,0:T(8,128)} %param.41) | copy-start | bytes 3145732
  1351.4 131.5 %copy-start.51 = (f32[47,47]{1,0:T(8,128)S(1)}, f32[47,47]{1,0:T(8,128)}, u32[]{:S(2)}) copy-start(f32[47,47]{1,0:T(8,128)} %param.42) | copy-start | bytes 26512
  1351.4 131.5 %copy-start.52 = (f32[512,47]{0,1:T(8,128)S(1)}, f32[512,47]{0,1:T(8,128)}, u32[]{:S(2)}) copy-start(f32[512,47]{0,1:T(8,128)} %param.45) | copy-start | bytes 288772
  1351.4 131.5 %copy-start.53 = (f32[512,47]{0,1:T(8,128)S(1)}, f32[512,47]{0,1:T(8,128)}, u32[]{:S(2)}) copy-start(f32[512,47]{0,1:T(8,128)} %param.48) | copy-start | bytes 288772
  1352.5 131.9 %copy-start.34 = (f32[512,47]{0,1:T(8,128)S(1)}, f32[512,47]{0,1:T(8,128)}, u32[]{:S(2)}) copy-start(f32[512,47]{0,1:T(8,128)} %param.36) | copy-start | bytes 288772
  1352.5 132.8 %copy-start.46 = (f32[200,200]{1,0:T(8,128)S(1)}, f32[200,200]{1,0:T(8,128)}, u32[]{:S(2)}) copy-start(f32[200,200]{1,0:T(8,128)} %param.37) | copy-start | bytes 480004
  1352.5 134.3 %copy-start.25 = (f32[256,256]{1,0:T(8,128)S(1)}, f32[256,256]{1,0:T(8,128)}, u32[]{:S(2)}) copy-start(f32[256,256]{1,0:T(8,128)} %param.38) | copy-start | bytes 786436
  1352.5 134.3 %copy-start.42 = (f32[200,256]{1,0:T(8,128)S(1)}, f32[200,256]{1,0:T(8,128)}, u32[]{:S(2)}) copy-start(f32[200,256]{1,0:T(8,128)} %param.43) | copy-start | bytes 614404
  1352.5 134.3 %copy-start.43 = (f32[200,256]{1,0:T(8,128)S(1)}, f32[200,256]{1,0:T(8,128)}, u32[]{:S(2)}) copy-start(f32[200,256]{1,0:T(8,128)} %param.46) | copy-start | bytes 614404
  1353.0 134.7 %copy-start.28 = (f32[200,256]{1,0:T(8,128)S(1)}, f32[200,256]{1,0:T(8,128)}, u32[]{:S(2)}) copy-start(f32[200,256]{1,0:T(8,128)} %param.34) | copy-start | bytes 614404
  1481.2 7.6 copy-start.32
  1482.9 7.0 copy-start.27
  1482.9 7.0 copy-start.30
  1482.9 7.0 copy-start.31
  1483.2 7.7 copy-start.35
  1483.2 7.7 copy-start.36
  1487.2 5.8 copy-start.44
  1487.2 5.8 copy-start.45
  1487.6 5.4 copy-start.19
  1490.9 3.9 copy-start.20
  (11 other events, 26.0 us)
Sparse Core Ops, SparseCore 0:
  1353.8 127.2 all-reduce.3
where the time goes:
time: 1520 us; the launch traced here: 1500 us
  local copies, waits for them, and re-layouts  742 us (49%)
  other arithmetic  478 us (31%)
  waiting for transfers between devices  113 us (7%)
  blocking collectives  77.7 us (5%)
  matrix products  53.1 us (3%)
  starting transfers between devices  23.7 us (2%)
  between operations  15.5 us (1%)
    gather x3, local copies, waits for them, and re-layouts, layer_forward(): picked = lookup[neighbors.reshape(-1)].reshape(local_rows, fanout, in_width)  488 us
    scatter-add x2, other arithmetic, layer_backward(): jnp.zeros((lookup.shape[0], in_width), jnp.float32)  333 us
    convert_element_type x3, local copies, waits for them, and re-layouts, layer_forward(): summed = jnp.sum(picked.astype(jnp.float32), axis=1)  89.1 us
    psum x1, waiting for transfers between devices, on_device(): lax.psum((grad_weights[0], grad_weights[1], grad_weights[2], grad_bias_al...  87.9 us
    reshape x2, local copies, waits for them, and re-layouts, layer_backward(): jnp.broadcast_to(grad_mean[:, None, :], (local_rows, fanout, in_width))  83.3 us
    reduce_sum x3, other arithmetic, layer_forward(): summed = jnp.sum(picked.astype(jnp.float32), axis=1)  73.7 us
    psum x1, blocking collectives, on_device(): lax.psum((grad_weights[0], grad_weights[1], grad_weights[2], grad_bias_al...  38.9 us
    psum x1, blocking collectives, on_device(): lax.psum((local_loss, jnp.sum(seed_float)), ('dom', 'rep'))  38.8 us
  transfers between devices with their start and end apart: 6, of which 5 were waited for; matrix products, arithmetic and copies ran while one was open for 3% of the time, Pallas kernels for 0%

commit v1 on v0

v1 whole, which is shorter than its diff:
```python
import functools

import jax
import jax.numpy as jnp
from jax import lax
from jax.experimental import pallas as pl
from jax.experimental.pallas import tpu as pltpu
from jax.sharding import PartitionSpec as P

STEP = 10


beta_one = 0.9
beta_two = 0.999
epsilon = 1e-08
step_rates = (0.05, 0.5, 1.0)
bias_rate = 0.05
weight_decay = 0.01

axes = ("dom", "rep")
WORDS = 4
SLOTS = 8
GROUPS = WORDS * SLOTS
BLOCK = 512
VMEM_BYTES = 56 * 1024 * 1024
TRANS_LEFT = (((0,), (0,)), ((), ()))
TRANS_RIGHT = (((1,), (1,)), ((), ()))


def dot(left, right, dims=(((1,), (0,)), ((), ()))):
    return lax.dot_general(left, right, dims, preferred_element_type=jnp.float32)


def params():
    return pltpu.CompilerParams(
        dimension_semantics=("arbitrary",), vmem_limit_bytes=VMEM_BYTES
    )


def whole(shape):
    return pl.BlockSpec(shape, lambda i: (0,) * len(shape))


def lanes(rows, width):
    return pl.BlockSpec((rows, width), lambda i: (0, i))


def words_layer(near_ref, out_ref, place_ref, field_ref):
    fanout, block = near_ref.shape
    span = out_ref.shape[0] // WORDS
    near = near_ref[...]
    group = ((near.astype(jnp.float32) + 0.5) * (1.0 / span)).astype(jnp.int32)
    place = near - group * span
    word = group >> 3
    bit = jnp.left_shift(jnp.int32(1), (group & 7) * 4)
    parts = [jnp.where(word == k, bit, 0) for k in range(WORDS)]
    totals = [jnp.zeros_like(bit) for _ in range(WORDS)]
    for g in range(fanout):
        same = place == place[g : g + 1]
        for k in range(WORDS):
            totals[k] = totals[k] + jnp.where(same, parts[k][g : g + 1], 0)
    place_ref[:fanout, :] = place
    for k in range(WORDS):
        field_ref[k, :fanout, :] = totals[k]
    chunk = 48
    for tile in range(0, block, 128):
        cols = slice(tile, tile + 128)
        for start in range(0, span, chunk):
            rows = lax.broadcasted_iota(jnp.int32, (chunk, 128), 0) + start
            sums = [jnp.zeros((chunk, 128), jnp.int32) for _ in range(WORDS)]
            for g in range(fanout):
                hit = rows == place_ref[g : g + 1, cols]
                for k in range(WORDS):
                    sums[k] = jnp.where(hit, field_ref[k, g : g + 1, cols], sums[k])
            for k in range(WORDS):
                out_ref[k * span + start : k * span + start + chunk, cols] = sums[k]


def words_kernel(one_ref, two_ref, three_ref, out_one, out_two, out_three, place_ref, field_ref):
    words_layer(one_ref, out_one, place_ref, field_ref)
    words_layer(two_ref, out_two, place_ref, field_ref)
    words_layer(three_ref, out_three, place_ref, field_ref)


def count_words(near, table):
    nodes = near[0].shape[1]
    height = table // SLOTS
    return pl.pallas_call(
        words_kernel,
        grid=(nodes // BLOCK,),
        in_specs=[lanes(n.shape[0], BLOCK) for n in near],
        out_specs=[lanes(height, BLOCK)] * 3,
        out_shape=[jax.ShapeDtypeStruct((height, nodes), jnp.int32)] * 3,
        scratch_shapes=[
            pltpu.VMEM((16, BLOCK), jnp.int32),
            pltpu.VMEM((WORDS, 16, BLOCK), jnp.int32),
        ],
        compiler_params=params(),
        name="count_words",
    )(*near)


def field(words, slot):
    if slot == SLOTS - 1:
        picked = lax.shift_right_logical(words, 4 * slot)
    else:
        picked = words & (15 << (4 * slot))
    return picked.astype(jnp.float32).astype(jnp.bfloat16)


def slot_scale(slot):
    return 1.0 if slot == SLOTS - 1 else 2.0 ** (-4 * slot)


def spread_counts(words_ref, counts_ref, group, span):
    word, slot = divmod(group, SLOTS)
    width = words_ref.shape[1]
    for tile in range(0, width, 128):
        cols = slice(tile, tile + 128)
        for start in range(0, span, 48):
            counts_ref[group * span + start : group * span + start + 48, cols] = field(
                words_ref[word * span + start : word * span + start + 48, cols], slot
            )


def gather_product(table_ref, words_ref, counts_ref):
    table = table_ref.shape[1]
    span = table // GROUPS
    total = None
    done = 0
    step = 512
    for group in range(GROUPS):
        spread_counts(words_ref, counts_ref, group, span)
        ready = (group + 1) * span
        while ready - done >= step or (group == GROUPS - 1 and done < table):
            stop = min(done + step, table)
            term = dot(table_ref[:, done:stop], counts_ref[done:stop, :])
            total = term if total is None else total + term
            done = stop
    return total


def scaled_table(own, got, scale, table_ref):
    width, nodes = own.shape
    table_ref[:width, :nodes] = (own.astype(jnp.float32) * scale[:, :nodes]).astype(jnp.bfloat16)
    table_ref[:width, nodes:] = (got.astype(jnp.float32) * scale[:, nodes:]).astype(jnp.bfloat16)


def hidden_kernel(
    fanout,
    words_ref,
    own_ref,
    own_block,
    got_ref,
    scale_ref,
    self_ref,
    near_ref,
    bias_ref,
    send_ref,
    state_ref,
    preact_ref,
    sent_ref,
    extra_ref,
    table_ref,
    counts_ref,
    picked_ref,
):
    step = pl.program_id(0)
    width = own_ref.shape[0]

    @pl.when(step == 0)
    def _():
        if table_ref.shape[0] > width:
            table_ref[...] = jnp.zeros_like(table_ref)
        got = got_ref[...].T
        scaled_table(own_ref[...], got, scale_ref[...], table_ref)
        if width == state_ref.shape[0]:
            extra_ref[:, : own_ref.shape[1]] = own_ref[...]
            extra_ref[:, own_ref.shape[1] :] = got
        picked_ref[...] = jnp.zeros_like(picked_ref)

    mean = (gather_product(table_ref, words_ref, counts_ref) / fanout).astype(jnp.bfloat16)
    if width != state_ref.shape[0]:
        extra_ref[...] = mean
    preact = dot(self_ref[...], own_block[...]) + dot(near_ref[...], mean) + bias_ref[...]
    preact_ref[...] = preact
    active = preact * jax.nn.sigmoid(preact)
    norm = lax.rsqrt(jnp.sum(active * active, axis=0, keepdims=True) + 1e-06)
    state = (active * norm).astype(jnp.bfloat16)
    state_ref[...] = state
    block = state.shape[1]
    node = lax.broadcasted_iota(jnp.int32, (1, block), 1) + step * block
    chosen = jnp.where(send_ref[...] == node, 1.0, 0.0).astype(jnp.bfloat16)
    picked_ref[...] += dot(chosen, state, TRANS_RIGHT)

    @pl.when(step == pl.num_programs(0) - 1)
    def _():
        sent_ref[...] = picked_ref[...].astype(jnp.bfloat16)


def hidden_layer(words, own, got, scale, weight_self, weight_near, bias_col, send_col, fanout):
    width, nodes = own.shape
    halo = got.shape[0]
    table = nodes + halo
    units = weight_self.shape[0]
    padded = weight_near.shape[1]
    if width == units:
        extra_shape, extra_spec = (units, table), whole((units, table))
    else:
        extra_shape, extra_spec = (padded, nodes), lanes(padded, BLOCK)
    return pl.pallas_call(
        functools.partial(hidden_kernel, fanout),
        grid=(nodes // BLOCK,),
        in_specs=[
            lanes(words.shape[0], BLOCK),
            whole(own.shape),
            lanes(width, BLOCK),
            whole(got.shape),
            whole(scale.shape),
            whole(weight_self.shape),
            whole(weight_near.shape),
            whole(bias_col.shape),
            whole(send_col.shape),
        ],
        out_specs=[
            lanes(units, BLOCK),
            lanes(units, BLOCK),
            whole((halo, units)),
            extra_spec,
        ],
        out_shape=[
            jax.ShapeDtypeStruct((units, nodes), jnp.bfloat16),
            jax.ShapeDtypeStruct((units, nodes), jnp.float32),
            jax.ShapeDtypeStruct((halo, units), jnp.bfloat16),
            jax.ShapeDtypeStruct(extra_shape, jnp.bfloat16),
        ],
        scratch_shapes=[
            pltpu.VMEM((padded, table), jnp.bfloat16),
            pltpu.VMEM((table, BLOCK), jnp.bfloat16),
            pltpu.VMEM((halo, units), jnp.float32),
        ],
        compiler_params=params(),
        name="hidden_layer",
    )(words, own, own, got, scale, weight_self, weight_near, bias_col, send_col)


def seed_kernel(rows_ref, labels_ref, mask_ref, out_ref):
    step = pl.program_id(0)
    classes, block = out_ref.shape
    slots = rows_ref.shape[0]
    kind = lax.broadcasted_iota(jnp.int32, (classes, slots), 0)
    marked = jnp.where((kind == labels_ref[...]) & (mask_ref[...] != 0), 1.0, 0.0)
    node = lax.broadcasted_iota(jnp.int32, (1, block), 1) + step * block
    chosen = jnp.where(rows_ref[...] == node, 1.0, 0.0).astype(jnp.bfloat16)
    out_ref[...] = dot(marked.astype(jnp.bfloat16), chosen)


def seed_counts(rows_col, labels_row, mask_row, nodes, classes):
    return pl.pallas_call(
        seed_kernel,
        grid=(nodes // BLOCK,),
        in_specs=[whole(rows_col.shape), whole(labels_row.shape), whole(mask_row.shape)],
        out_specs=lanes(classes, BLOCK),
        out_shape=jax.ShapeDtypeStruct((classes, nodes), jnp.float32),
        compiler_params=params(),
        name="seed_counts",
    )(rows_col, labels_row, mask_row)


def last_kernel(
    fanout,
    words_ref,
    own_ref,
    own_block,
    got_ref,
    scale_ref,
    self_ref,
    near_ref,
    bias_ref,
    seeds_ref,
    grad_ref,
    sums_ref,
    table_out,
    reduced_ref,
    counts_ref,
):
    step = pl.program_id(0)
    classes = self_ref.shape[0]
    nodes = own_ref.shape[1]

    @pl.when(step == 0)
    def _():
        table_out[:, :nodes] = own_ref[...]
        table_out[:, nodes:] = got_ref[...].T
        reduced = dot(near_ref[...], table_out[...]) * scale_ref[...]
        high = reduced.astype(jnp.bfloat16)
        reduced_ref[:classes, :] = high
        reduced_ref[classes:, :] = (reduced - high.astype(jnp.float32)).astype(jnp.bfloat16)
        sums_ref[...] = jnp.zeros_like(sums_ref)

    both = gather_product(reduced_ref, words_ref, counts_ref)
    near_part = (both[:classes] + both[classes:]) / fanout
    logits = dot(self_ref[...], own_block[...]) + near_part + bias_ref[...]
    top = jnp.max(logits, axis=0, keepdims=True)
    powers = jnp.exp(logits - top)
    total = jnp.sum(powers, axis=0, keepdims=True)
    normer = jnp.log(total) + top
    seeds = seeds_ref[...]
    uses = jnp.sum(seeds, axis=0, keepdims=True)
    grad = (powers / total * uses - seeds).astype(jnp.bfloat16)
    grad_ref[...] = grad
    loss = uses * normer - jnp.sum(seeds * logits, axis=0, keepdims=True)
    sums_ref[:classes, :] += jnp.sum(grad.astype(jnp.float32), axis=1, keepdims=True)
    sums_ref[classes:, :] += jnp.sum(loss)


def last_layer(words, own, got, scale, weight_self, weight_near, bias_col, seeds, fanout):
    width, nodes = own.shape
    table = nodes + got.shape[0]
    classes = weight_self.shape[0]
    return pl.pallas_call(
        functools.partial(last_kernel, fanout),
        grid=(nodes // BLOCK,),
        in_specs=[
            lanes(words.shape[0], BLOCK),
            whole(own.shape),
            lanes(width, BLOCK),
            whole(got.shape),
            whole(scale.shape),
            whole(weight_self.shape),
            whole(weight_near.shape),
            whole(bias_col.shape),
            lanes(classes, BLOCK),
        ],
        out_specs=[
            lanes(classes, BLOCK),
            whole((classes + 8, 128)),
            whole((width, table)),
        ],
        out_shape=[
            jax.ShapeDtypeStruct((classes, nodes), jnp.bfloat16),
            jax.ShapeDtypeStruct((classes + 8, 128), jnp.float32),
            jax.ShapeDtypeStruct((width, table), jnp.bfloat16),
        ],
        scratch_shapes=[
            pltpu.VMEM((2 * classes, table), jnp.bfloat16),
            pltpu.VMEM((table, BLOCK), jnp.bfloat16),
        ],
        compiler_params=params(),
        name="last_layer",
    )(words, own, own, got, scale, weight_self, weight_near, bias_col, seeds)


def scatter_kernel(
    fanout,
    words_ref,
    grad_ref,
    table_ref,
    self_ref,
    near_ref,
    state_ref,
    weight_ref,
    rows_ref,
    padded_ref,
    counts_ref,
    sums_ref,
):
    step = pl.program_id(0)
    units, nodes = grad_ref.shape
    span = words_ref.shape[0]
    part = span * SLOTS

    @pl.when(step == 0)
    def _():
        rows_ref[...] = grad_ref[...].T
        for k in range(WORDS):
            start = k * part
            stop = min(start + part, nodes)
            if stop > start:
                padded_ref[k, :, : stop - start] = grad_ref[:, start:stop]
            if stop < start + part:
                left = max(stop - start, 0)
                padded_ref[k, :, left:] = jnp.zeros((units, part - left), jnp.bfloat16)
        weight_ref[...] = jnp.zeros_like(weight_ref)

    pair = 2
    for slot in range(0, SLOTS, pair):
        for one in range(slot, slot + pair):
            spread_slot(words_ref, counts_ref, one, span)
        added = dot(counts_ref[slot * span : (slot + pair) * span, :], rows_ref[...])
        for one in range(slot, slot + pair):
            piece = added[(one - slot) * span : (one - slot + 1) * span, :]
            sums_ref[one * span : (one + 1) * span, :] = (
                piece * (slot_scale(one) / fanout)
            ).astype(jnp.bfloat16)
    sums = sums_ref[...]
    own_grad = padded_ref[step]
    state_ref[...] = dot(near_ref[...], sums, TRANS_RIGHT) + dot(self_ref[...], own_grad)
    width = table_ref.shape[0]
    weight_ref[:width, :] += dot(table_ref[...], own_grad, TRANS_RIGHT)
    weight_ref[width:, :] += dot(table_ref[...], sums)


def spread_slot(words_ref, counts_ref, slot, span):
    for tile in range(0, words_ref.shape[1], 128):
        cols = slice(tile, tile + 128)
        for start in range(0, span, 48):
            counts_ref[slot * span + start : slot * span + start + 48, cols] = field(
                words_ref[start : start + 48, cols], slot
            )


def scatter_layer(words, grad, table, weight_self, weight_near, fanout):
    units, nodes = grad.shape
    width, rows = table.shape
    span = rows // GROUPS
    part = rows // WORDS
    return pl.pallas_call(
        functools.partial(scatter_kernel, fanout),
        grid=(WORDS,),
        in_specs=[
            pl.BlockSpec((span, nodes), lambda i: (i, 0)),
            whole(grad.shape),
            lanes(width, part),
            whole(weight_self.shape),
            whole(weight_near.shape),
        ],
        out_specs=[lanes(width, part), whole((2 * width, units))],
        out_shape=[
            jax.ShapeDtypeStruct((width, rows), jnp.float32),
            jax.ShapeDtypeStruct((2 * width, units), jnp.float32),
        ],
        scratch_shapes=[
            pltpu.VMEM((nodes, units), jnp.bfloat16),
            pltpu.VMEM((WORDS, units, part), jnp.bfloat16),
            pltpu.VMEM((part, nodes), jnp.bfloat16),
            pltpu.VMEM((part, units), jnp.bfloat16),
        ],
        compiler_params=params(),
        name="scatter_layer",
    )(words, grad, table, weight_self, weight_near)


def active_kernel(first, state_ref, preact_ref, returned_ref, send_ref, *refs):
    if first:
        own_block, mean_block, grad_ref, sums_ref, weight_ref = refs
    else:
        grad_ref, sums_ref = refs
    step = pl.program_id(0)
    block = state_ref.shape[1]
    node = lax.broadcasted_iota(jnp.int32, (1, block), 1) + step * block
    chosen = jnp.where(send_ref[...] == node, 1.0, 0.0).astype(jnp.bfloat16)
    upper = state_ref[...] + dot(returned_ref[...], chosen, TRANS_LEFT)
    preact = preact_ref[...]
    gate = jax.nn.sigmoid(preact)
    active = preact * gate
    norm = lax.rsqrt(jnp.sum(active * active, axis=0, keepdims=True) + 1e-06)
    along = jnp.sum(active * upper, axis=0, keepdims=True)
    inner = norm * upper - active * (norm * norm * norm * along)
    grad = (inner * (gate * (1.0 + preact * (1.0 - gate)))).astype(jnp.bfloat16)
    grad_ref[...] = grad

    @pl.when(step == 0)
    def _():
        sums_ref[...] = jnp.zeros_like(sums_ref)
        if first:
            weight_ref[...] = jnp.zeros_like(weight_ref)

    sums_ref[...] += jnp.sum(grad.astype(jnp.float32), axis=1, keepdims=True)
    if first:
        width = own_block.shape[0]
        weight_ref[0, :width, :] += dot(own_block[...], grad, TRANS_RIGHT)
        weight_ref[1] += dot(mean_block[...], grad, TRANS_RIGHT)


def active_layer(state_grad, preact, returned, send_col, own=None, mean=None):
    units, nodes = preact.shape
    first = own is not None
    in_specs = [
        lanes(units, BLOCK),
        lanes(units, BLOCK),
        whole(returned.shape),
        whole(send_col.shape),
    ]
    out_specs = [lanes(units, BLOCK), whole((units, 128))]
    out_shape = [
        jax.ShapeDtypeStruct((units, nodes), jnp.bfloat16),
        jax.ShapeDtypeStruct((units, 128), jnp.float32),
    ]
    operands = [state_grad, preact, returned, send_col]
    if first:
        padded = mean.shape[0]
        in_specs += [lanes(own.shape[0], BLOCK), lanes(padded, BLOCK)]
        out_specs.append(whole((2, padded, units)))
        out_shape.append(jax.ShapeDtypeStruct((2, padded, units), jnp.float32))
        operands += [own, mean]
    return pl.pallas_call(
        functools.partial(active_kernel, first),
        grid=(nodes // BLOCK,),
        in_specs=in_specs,
        out_specs=out_specs,
        out_shape=out_shape,
        compiler_params=params(),
        name="active_layer",
    )(*operands)


def product(left, right):
    return jnp.dot(left, right, precision=lax.Precision.HIGHEST, preferred_element_type=jnp.float32)


def exchange(rows):
    return lax.all_to_all(rows, axes, split_axis=0, concat_axis=0, tiled=True)


def rotate_adam(weight, grad, first, second, left_basis, right_basis, rate):
    turned = product(product(left_basis.T, grad), right_basis)
    first = beta_one * first + (1.0 - beta_one) * turned
    second = beta_two * second + (1.0 - beta_two) * turned * turned
    update = first / (1.0 - beta_one**STEP) / (jnp.sqrt(second / (1.0 - beta_two**STEP)) + epsilon)
    return (weight - rate * product(product(left_basis, update), right_basis.T), first, second)


def on_device(
    features,
    labels,
    seed_rows,
    seed_mask,
    send_rows,
    neighbors_one,
    neighbors_two,
    neighbors_three,
    weight_one,
    weight_two,
    weight_three,
    left_one,
    right_one,
    left_two,
    right_two,
    left_three,
    right_three,
    first_one,
    first_two,
    first_three,
    second_one,
    second_two,
    second_three,
    bias_all,
    bias_first,
    bias_second,
):
    nodes, width = features.shape
    units = weight_one.shape[1]
    classes = weight_three.shape[1]
    halo = send_rows.size
    table = nodes + halo
    span = table // GROUPS
    low = jnp.bfloat16
    fans = (neighbors_one.shape[1], neighbors_two.shape[1], neighbors_three.shape[1])
    near = (neighbors_one.T, neighbors_two.T, neighbors_three.T)
    feats = features.T
    slot_of = (jnp.arange(table, dtype=jnp.int32) // span) % SLOTS
    scale = jnp.where(slot_of == SLOTS - 1, 1.0, 0.0)
    for slot in range(SLOTS - 1):
        scale = jnp.where(slot_of == slot, slot_scale(slot), scale)
    scale = scale.astype(jnp.float32)[None, :]
    send_col = send_rows.reshape(halo, 1)

    got_one = exchange(features[send_rows.reshape(-1)])
    words = count_words(near, table)
    padded_classes = -(-classes // 16) * 16
    more = padded_classes - classes
    seeds = seed_counts(
        seed_rows.reshape(-1, 1),
        labels.reshape(1, -1),
        seed_mask.reshape(1, -1),
        nodes,
        padded_classes,
    )
    seed_float = seed_mask.astype(jnp.float32)

    padded = -(-width // 16) * 16
    self_one = weight_one[:width].T.astype(low)
    near_one = jnp.pad(weight_one[width:].T, ((0, 0), (0, padded - width))).astype(low)
    self_two = weight_two[:units].astype(low)
    near_two = weight_two[units:].astype(low)
    wide_three = jnp.pad(weight_three, ((0, 0), (0, more))).astype(low)
    self_three = wide_three[:units]
    near_three = wide_three[units:]
    bias_three = jnp.pad(bias_all[2 * units :], (0, more), constant_values=-1e30)

    state_one, preact_one, sent_two, mean_one = hidden_layer(
        words[0],
        feats,
        got_one,
        scale,
        self_one,
        near_one,
        bias_all[:units].reshape(-1, 1),
        send_col,
        fans[0],
    )
    got_two = exchange(sent_two)
    state_two, preact_two, sent_three, table_two = hidden_layer(
        words[1],
        state_one,
        got_two,
        scale,
        self_two.T,
        near_two.T,
        bias_all[units : 2 * units].reshape(-1, 1),
        send_col,
        fans[1],
    )
    got_three = exchange(sent_three)
    grad_three, sums_three, table_three = last_layer(
        words[2],
        state_two,
        got_three,
        scale,
        self_three.T,
        near_three.T,
        bias_three.reshape(-1, 1),
        seeds,
        fans[2],
    )
    state_grad, weight_grad_three = scatter_layer(
        words[2], grad_three, table_three, self_three, near_three, fans[2]
    )
    returned = exchange(state_grad[:, nodes:].T.astype(low))
    grad_two, sums_two = active_layer(state_grad, preact_two, returned, send_col)
    state_grad, weight_grad_two = scatter_layer(
        words[1], grad_two, table_two, self_two, near_two, fans[1]
    )
    returned = exchange(state_grad[:, nodes:].T.astype(low))
    _, sums_one, weight_grad_one = active_layer(
        state_grad, preact_one, returned, send_col, feats, mean_one
    )
    small = jnp.concatenate(
        [
            sums_one[:, 0],
            sums_two[:, 0],
            sums_three[:classes, 0],
            sums_three[padded_classes : padded_classes + 1, 0],
            jnp.sum(seed_float)[None],
        ]
    )
    weight_grad_one = weight_grad_one[:, :width].reshape(2 * width, units)
    summed = lax.psum((weight_grad_one, weight_grad_two, weight_grad_three, small), axes)
    loss_sum = summed[3][-2]
    seed_total = summed[3][-1]
    share = 1.0 / seed_total
    bias_grad = summed[3][:-2] * share
    out_one = rotate_adam(
        weight_one, summed[0] * share, first_one, second_one, left_one, right_one, step_rates[0]
    )
    out_two = rotate_adam(
        weight_two, summed[1] * share, first_two, second_two, left_two, right_two, step_rates[1]
    )
    out_three = rotate_adam(
        weight_three,
        summed[2][:, :classes] * share,
        first_three,
        second_three,
        left_three,
        right_three,
        step_rates[2],
    )
    bias_m = beta_one * bias_first + (1.0 - beta_one) * bias_grad
    bias_v = beta_two * bias_second + (1.0 - beta_two) * bias_grad * bias_grad
    bias_update = (
        bias_m / (1.0 - beta_one**STEP) / (jnp.sqrt(bias_v / (1.0 - beta_two**STEP)) + epsilon)
    )
    new_bias = bias_all - bias_rate * (bias_update + weight_decay * bias_all)
    return (*out_one, *out_two, *out_three, new_bias, bias_m, bias_v, loss_sum, seed_total)


def solution(mesh):
    split = P(axes)
    rows = P(axes, None)
    placed = (rows, split, split, split, rows, rows, rows, rows) + (P(),) * 18
    return jax.shard_map(
        on_device,
        mesh=mesh,
        in_specs=placed,
        out_specs=(P(),) * 14,
        check_vma=False,
    )
```

time: 1520 us -> 383 us (0.25); the launches traced: 1500 us -> 382 us
  local copies, waits for them, and re-layouts: 742 us -> 29.2 us
  other arithmetic: 478 us -> 2.03 us
  Pallas kernels: 0 us -> 147 us
  matrix products: 53.1 us -> 14.5 us
  blocking collectives: 77.7 us -> 54.8 us
    gather x7 -> x1, local copies, waits for them, and re-layouts: 502 us -> 1.92 us  [on_device(): got_one = exchange(features[send_rows.reshape(-1)])]
    scatter-add x5 -> x0, other arithmetic: 362 us -> none  [the longest x2 333 us: layer_backward(): jnp.zeros((lookup.shape[0], in_width), jnp.float32)]
    pallas_call x0 -> x9, Pallas kernels: none -> 147 us  [the longest x2 45.5 us: hidden_layer(): pl.pallas_call(functools.partial(hidden_kernel, fanout), grid=(nodes // B...]
    reduce_sum x10 -> x1, other arithmetic: 95.3 us -> 0.6 us  [on_device(): jnp.sum(seed_float)[None]]
    reshape x6 -> x8, local copies, waits for them, and re-layouts: 93.8 us -> 5.31 us  [the longest x1 1.38 us: on_device(): seed_rows.reshape(-1, 1)]
    convert_element_type x3 -> x4, local copies, waits for them, and re-layouts: 89.1 us -> 3.12 us  [on_device(): returned = exchange(state_grad[:, nodes:].T.astype(low))]
    dot_general x16 -> x0, matrix products: 39.8 us -> none  [the longest x3 13.6 us: layer_forward(): jnp.dot(mean, weight_low[in_width:], preferred_element_type=jnp.float32)]
    psum x2 -> x1, blocking collectives: 77.7 us -> 38.7 us  [on_device(): lax.psum((weight_grad_one, weight_grad_two, weight_grad_three, small), axes)]
  transfers between devices with their start and end apart: 6 -> 5, of which waited for: 5 -> 3; matrix products, arithmetic and copies ran while one was open for 3% -> 5% of each run, Pallas kernels for 0% -> 7%
where the time goes in v1:
time: 383 us; the launch traced here: 382 us
  Pallas kernels  147 us (38%)
  waiting for transfers between devices  100 us (26%)
  blocking collectives  54.8 us (14%)
  local copies, waits for them, and re-layouts  29.2 us (8%)
  starting transfers between devices  18.8 us (5%)
  between operations  15.2 us (4%)
  matrix products  14.5 us (4%)
    psum x1, waiting for transfers between devices, on_device(): lax.psum((weight_grad_one, weight_grad_two, weight_grad_three, small), axes)  84.4 us
    pallas_call x2, Pallas kernels, hidden_layer(): pl.pallas_call(functools.partial(hidden_kernel, fanout), grid=(nodes // B...  45.5 us
    psum x1, blocking collectives, on_device(): lax.psum((weight_grad_one, weight_grad_two, weight_grad_three, small), axes)  38.7 us
    pallas_call x2, Pallas kernels, scatter_layer(): pl.pallas_call(functools.partial(scatter_kernel, fanout), grid=(WORDS,),...  34.1 us
    pallas_call x1, Pallas kernels, count_words(): pl.pallas_call(words_kernel, grid=(nodes // BLOCK,), in_specs=[lanes(n.sh...  21.3 us
    pallas_call x2, Pallas kernels, active_layer(): pl.pallas_call(functools.partial(active_kernel, first), grid=(nodes // BL...  20.6 us
    pallas_call x1, Pallas kernels, last_layer(): pl.pallas_call(functools.partial(last_kernel, fanout), grid=(nodes // BLO...  19.1 us
    all_to_all x4, starting transfers between devices, exchange(): return lax.all_to_all(rows, axes, split_axis=0, concat_axis=0, tiled=True)  18.5 us
  transfers between devices with their start and end apart: 5, of which 3 were waited for; matrix products, arithmetic and copies ran while one was open for 5% of the time, Pallas kernels for 7%

profile of v1, /device:TPU:0, one launch (start us, length us, event | category | flops | bytes accessed | tf_op | source)
XLA Modules:
  0.0 382.1 jit_solution(3097601814736509524)
XLA Ops:
  7.2 0.9 copy.69
  8.2 1.6 copy.70
  9.8 1.9 gather_fusion
  11.7 7.3 %all-to-all-start = ((bf16[32,16,100]{2,1,0:T(8,128)(2,1)}), bf16[32,16,100]{2,1,0:T(8,128)(2,1)S(1)}, u32[]{:S(2)}, u32[]{:S(2)}) async-start(bf16[32,16,100]{2,1,0:T(8,128)(2,1)} %bitcast.5), calls=%async_computation | async-start | bytes 262144 | tf_op jit(solution)/shard_map/all_to_all | solution.py:513
  19.0 0.9 copy.73.send_ref
  19.9 0.8 compare_select_fusion.9.scale_ref
  20.6 1.0 copy.71
  21.6 0.8 fusion.58
  22.4 0.8 copy.72.bias_ref
  23.2 0.7 slice_bitcast_fusion
  23.9 0.6 pad.14.near_ref
  24.5 21.3 %count_words.1 = (s32[576,4096]{1,0:T(8,128)}, s32[576,4096]{1,0:T(8,128)}, s32[576,4096]{1,0:T(8,128)}) custom-call(s32[15,4096]{1,0:T(8,128)} %bitcast.69, s32[10,4096]{1,0:T(8,128)} %bitcast.70, s32[5,4096]{1,0:T(8,128)} %bitcast.73), custom_call_target="tpu_custom_call" | custom-call | tf_op jit(solution)/shard_map/count_words/pallas_call | solution.py:88
  45.8 0.7 copy-done.11
  46.5 22.7 %hidden_layer.2 = (bf16[256,4096]{1,0:T(8,128)(2,1)}, f32[256,4096]{1,0:T(8,128)}, bf16[512,256]{1,0:T(8,128)(2,1)}, bf16[112,4096]{1,0:T(8,128)(2,1)}) custom-call(s32[576,4096]{1,0:T(8,128)} %get-tuple-element.38.words_ref, bf16[100,4096]{1,0:T(8,128)(2,1)} %bitcast.60, bf16[100,4096]{1,0:T(8,128)(2,1)} %bitcast.61, bf16[512,100]{1,0:T(8,128)(2,1)} %bitcast.68, ...), custom_call_target="tpu_custom_call" | custom-call | tf_op jit(solution)/shard_map/hidden_layer/pallas_call | solution.py:211
  69.2 5.8 %all-to-all-start.1 = ((bf16[32,16,256]{2,1,0:T(8,128)(2,1)}), bf16[32,16,256]{2,1,0:T(8,128)(2,1)S(1)}, u32[]{:S(2)}, u32[]{:S(2)}) async-start(bf16[32,16,256]{2,1,0:T(8,128)(2,1)} %bitcast.72), calls=%async_computation.1 | async-start | bytes 524288 | tf_op jit(solution)/shard_map/all_to_all | solution.py:513
  75.1 0.7 fusion.56
  75.8 0.8 copy.74.self_ref
  76.5 0.8 copy.75.near_ref
  77.3 0.8 copy.76.bias_ref
  78.1 7.5 %all-to-all-done.1 = bf16[32,16,256]{2,1,0:T(8,128)(2,1)S(1)} async-done(((bf16[32,16,256]{2,1,0:T(8,128)(2,1)}), bf16[32,16,256]{2,1,0:T(8,128)(2,1)S(1)}, u32[]{:S(2)}, u32[]{:S(2)}) %all-to-all-start.1) | async-done | bytes 262176 | tf_op jit(solution)/shard_map/all_to_all | solution.py:513
  85.6 0.7 copy-done.6
  86.3 22.8 %hidden_layer.3 = (bf16[256,4096]{1,0:T(8,128)(2,1)}, f32[256,4096]{1,0:T(8,128)}, bf16[512,256]{1,0:T(8,128)(2,1)}, bf16[256,4608]{1,0:T(8,128)(2,1)}) custom-call(s32[576,4096]{1,0:T(8,128)} %get-tuple-element.36.words_ref, bf16[256,4096]{1,0:T(8,128)(2,1)} %get-tuple-element.39.own_ref.own_block, bf16[256,4096]{1,0:T(8,128)(2,1)} %get-tuple-element.39.own_ref.own_block, ...), custom_call_target="tpu_custom_call" | custom-call | tf_op jit(solution)/shard_map/hidden_layer/pallas_call | solution.py:211
  109.1 2.8 all-to-all-start.2
  112.1 0.7 pad_slice_fusion
  112.8 0.7 copy.80.self_ref
  113.5 0.7 copy.81.near_ref
  114.2 1.4 copy.79.rows_ref
  115.5 0.7 copy.82.bias_ref
  116.2 6.7 %seed_counts.1.seeds_ref = f32[48,4096]{1,0:T(8,128)} custom-call(s32[2048,1]{1,0:T(8,128)} %copy.79.rows_ref, s32[1,2048]{1,0:T(1,128)} %bitcast.76, s32[1,2048]{1,0:T(1,128)} %bitcast.74), custom_call_target="tpu_custom_call" | custom-call | tf_op jit(solution)/shard_map/seed_counts/pallas_call | solution.py:259
  122.9 0.7 copy-done.5
  123.6 19.1 %last_layer.1 = (bf16[48,4096]{1,0:T(8,128)(2,1)}, f32[56,128]{1,0:T(8,128)}, bf16[256,4608]{1,0:T(8,128)(2,1)}) custom-call(s32[576,4096]{1,0:T(8,128)} %get-tuple-element.37.words_ref, bf16[256,4096]{1,0:T(8,128)(2,1)} %get-tuple-element.41.own_ref.own_block, bf16[256,4096]{1,0:T(8,128)(2,1)} %get-tuple-element.41.own_ref.own_block, ...), custom_call_target="tpu_custom_call" | custom-call | tf_op jit(solution)/shard_map/last_layer/pallas_call | solution.py:321
  142.7 16.4 %scatter_layer.2 = (f32[256,4608]{1,0:T(8,128)}, f32[512,48]{1,0:T(8,128)}) custom-call(s32[576,4096]{1,0:T(8,128)} %get-tuple-element.37.words_ref, bf16[48,4096]{1,0:T(8,128)(2,1)} %get-tuple-element.43.grad_ref, bf16[256,4608]{1,0:T(8,128)(2,1)} %get-tuple-element.44.table_ref, bf16[256,48]{1,0:T(8,128)(2,1)} %get-tuple-element.75.self_ref, ...), custom_call_target="tpu_custom_call" | custom-call | tf_op jit(solution)/shard_map/scatter_layer/pallas_call | solution.py:418
  159.0 1.1 fusion.11
  160.3 16.2 %all_to_all.55 = bf16[32,16,256]{2,1,0:T(8,128)(2,1)} all-to-all(bf16[32,16,256]{2,1,0:T(8,128)(2,1)S(1)} %bitcast.67), channel_id=1, replica_groups=mesh['dom'=8,'rep'=4] {'dom','rep'}, dimensions={0} | all-to-all | bytes 524288 | tf_op jit(solution)/shard_map/all_to_all | solution.py:513
  176.4 9.6 %active_layer.2 = (bf16[256,4096]{1,0:T(8,128)(2,1)}, f32[256,128]{1,0:T(8,128)}) custom-call(f32[256,4608]{1,0:T(8,128)} %get-tuple-element.45.state_ref, f32[256,4096]{1,0:T(8,128)} %get-tuple-element.46.preact_ref, bf16[512,256]{1,0:T(8,128)(2,1)} %bitcast.66, s32[512,1]{1,0:T(8,128)} %copy.73.send_ref), custom_call_target="tpu_custom_call" | custom-call | tf_op jit(solution)/shard_map/active_layer/pallas_call | solution.py:497
  186.0 17.7 %scatter_layer.3 = (f32[256,4608]{1,0:T(8,128)}, f32[512,256]{1,0:T(8,128)}) custom-call(s32[576,4096]{1,0:T(8,128)} %get-tuple-element.36.words_ref, bf16[256,4096]{1,0:T(8,128)(2,1)} %get-tuple-element.47.grad_ref, bf16[256,4608]{1,0:T(8,128)(2,1)} %get-tuple-element.48.table_ref, bf16[256,256]{1,0:T(8,128)(2,1)} %get-tuple-element.69.self_ref, ...), custom_call_target="tpu_custom_call" | custom-call | tf_op jit(solution)/shard_map/scatter_layer/pallas_call | solution.py:418
  203.8 1.1 fusion.12
  204.8 0.8 copy.85
  205.7 2.6 all-to-all-start.4
  208.5 0.6 convert_reduce_fusion
  209.1 0.5 slice.81
  209.7 0.6 slice_reduce_fusion.2
  210.3 8.6 %all-to-all-done.4 = bf16[32,16,256]{2,1,0:T(8,128)(2,1)S(1)} async-done(((bf16[32,16,256]{2,1,0:T(8,128)(2,1)}), bf16[32,16,256]{2,1,0:T(8,128)(2,1)S(1)}, u32[]{:S(2)}, u32[]{:S(2)}) %all-to-all-start.4) | async-done | bytes 262176 | tf_op jit(solution)/shard_map/all_to_all | solution.py:513
  218.9 0.7 copy-done.8
  219.6 11.0 %active_layer.3 = (bf16[256,4096]{1,0:T(8,128)(2,1)}, f32[256,128]{1,0:T(8,128)}, f32[2,112,256]{2,1,0:T(8,128)}) custom-call(f32[256,4608]{1,0:T(8,128)} %get-tuple-element.49.state_ref, f32[256,4096]{1,0:T(8,128)} %get-tuple-element.50.preact_ref, bf16[512,256]{1,0:T(8,128)(2,1)} %bitcast.65, s32[512,1]{1,0:T(8,128)} %copy.73.send_ref, ...), custom_call_target="tpu_custom_call" | custom-call | tf_op jit(solution)/shard_map/active_layer/pallas_call | solution.py:497
  230.6 1.0 slice.77
  231.6 0.7 reshape.213
  232.3 1.2 slice_reduce_fusion
  233.5 2.0 concatenate.3
  235.5 38.7 %psum.29 = f32[561]{0:T(1024)S(1)} all-reduce(f32[561]{0:T(1024)S(1)} %concatenate.3), channel_id=1, replica_groups=mesh['dom'=8,'rep'=4] {'dom','rep'}, use_global_device_ids=true, to_apply=%region_2.3 | all-reduce | flops 561 | bytes 4488 | tf_op jit(solution)/shard_map/psum | solution.py:649
  274.2 0.6 fusion.57
  275.5 0.6 multiply_subtract_fusion
  276.1 84.4 %all-reduce.6.cloned.1.call-done = (f32[200,256]{1,0:T(8,128)}, f32[512,256]{1,0:T(8,128)}, f32[512,48]{1,0:T(8,128)}) async-done(((f32[200,256]{1,0:T(8,128)}, f32[512,256]{1,0:T(8,128)}, f32[512,48]{1,0:T(8,128)}), (f32[200,256]{1,0:T(8,128)}, f32[512,256]{1,0:T(8,128)}, f32[512,48]{1,0:T(8,128)})) %all-reduce.6.cloned.1.call-update) | async-done | bytes 827408 | tf_op jit(solution)/shard_map/psum | solution.py:649
  360.5 1.7 fusion.13
  362.2 1.2 multiply_add_fusion.2
  363.5 1.1 fusion.33
  364.6 0.9 convolution_subtract_fusion
  365.5 2.1 fusion.9
  367.7 1.0 multiply_add_fusion
  368.8 2.1 fusion.3
  370.9 1.8 fusion
  372.7 0.6 fusion.25
  373.7 0.4 fusion.19
  374.2 1.1 fusion.1
  (70 shorter events, 1.2 us)
Async XLA Ops:
  7.2 358.3 %copy-start = (f32[512,512]{1,0:T(8,128)S(1)}, f32[512,512]{1,0:T(8,128)}, u32[]{:S(2)}) copy-start(f32[512,512]{1,0:T(8,128)} %param.39) | copy-start | bytes 3145732
  11.7 34.1 %all-to-all-start = ((bf16[32,16,100]{2,1,0:T(8,128)(2,1)}), bf16[32,16,100]{2,1,0:T(8,128)(2,1)S(1)}, u32[]{:S(2)}, u32[]{:S(2)}) async-start(bf16[32,16,100]{2,1,0:T(8,128)(2,1)} %bitcast.5), calls=%async_computation | async-start | bytes 262144 | tf_op jit(solution)/shard_map/all_to_all | solution.py:513
  45.8 0.7 copy-start.11
  46.5 28.6 %copy-start.2 = (f32[512,256]{1,0:T(8,128)S(1)}, f32[512,256]{1,0:T(8,128)}, u32[]{:S(2)}) copy-start(f32[512,256]{1,0:T(8,128)} %param.35) | copy-start | bytes 1572868
  69.2 16.4 %all-to-all-start.1 = ((bf16[32,16,256]{2,1,0:T(8,128)(2,1)}), bf16[32,16,256]{2,1,0:T(8,128)(2,1)S(1)}, u32[]{:S(2)}, u32[]{:S(2)}) async-start(bf16[32,16,256]{2,1,0:T(8,128)(2,1)} %bitcast.72), calls=%async_computation.1 | async-start | bytes 524288 | tf_op jit(solution)/shard_map/all_to_all | solution.py:513
  85.6 0.7 copy-start.6
  86.3 25.6 %copy-start.26 = (f32[559]{0:T(1024)S(1)}, f32[559]{0:T(1024)}, u32[]{:S(2)}) copy-start(f32[559]{0:T(1024)} %param.49) | copy-start | bytes 6712
  86.3 25.6 %copy-start.14 = (f32[512,47]{0,1:T(8,128)S(1)}, f32[512,47]{0,1:T(8,128)}, u32[]{:S(2)}) copy-start(f32[512,47]{0,1:T(8,128)} %param.36) | copy-start | bytes 288772
  86.3 27.9 %copy-start.27 = (s32[2048]{0:T(1024)S(1)}, s32[2048]{0:T(1024)}, u32[]{:S(2)}) copy-start(s32[2048]{0:T(1024)} %param.28) | copy-start | bytes 24580
  109.1 13.8 %all-to-all-start.2 = ((bf16[32,16,256]{2,1,0:T(8,128)(2,1)}), bf16[32,16,256]{2,1,0:T(8,128)(2,1)S(1)}, u32[]{:S(2)}, u32[]{:S(2)}) async-start(bf16[32,16,256]{2,1,0:T(8,128)(2,1)} %bitcast.71), calls=%async_computation.2 | async-start | bytes 524288 | tf_op jit(solution)/shard_map/all_to_all | solution.py:513
  122.9 0.7 copy-start.5
  186.0 22.5 %copy-start.24 = (s32[2048]{0:T(1024)S(1)}, s32[2048]{0:T(1024)}, u32[]{:S(2)}) copy-start(s32[2048]{0:T(1024)} %param.29) | copy-start | bytes 24580
  186.0 23.1 %copy-start.25 = (f32[56,128]{1,0:T(8,128)S(1)}, f32[56,128]{1,0:T(8,128)}, u32[]{:S(2)}) copy-start(f32[56,128]{1,0:T(8,128)} %get-tuple-element.55) | copy-start | bytes 86020
  205.7 13.2 %all-to-all-start.4 = ((bf16[32,16,256]{2,1,0:T(8,128)(2,1)}), bf16[32,16,256]{2,1,0:T(8,128)(2,1)S(1)}, u32[]{:S(2)}, u32[]{:S(2)}) async-start(bf16[32,16,256]{2,1,0:T(8,128)(2,1)} %bitcast.27), calls=%async_computation.4 | async-start | bytes 524288 | tf_op jit(solution)/shard_map/all_to_all | solution.py:513
  208.3 152.2 %all-reduce.6.cloned.1.call-start = ((), (), s32[]{:S(2)}) async-start(), calls=%async_computation.5 | async-start | bytes 1982464 | tf_op jit(solution)/shard_map/psum | solution.py:649
  218.9 0.7 copy-start.8
  219.6 55.9 %copy-start.28 = (f32[559]{0:T(1024)S(1)}, f32[559]{0:T(1024)}, u32[]{:S(2)}) copy-start(f32[559]{0:T(1024)} %param.50) | copy-start | bytes 6712
  219.6 55.9 %copy-start.29 = (f32[559]{0:T(1024)S(1)}, f32[559]{0:T(1024)}, u32[]{:S(2)}) copy-start(f32[559]{0:T(1024)} %param.51) | copy-start | bytes 6712
  219.6 140.9 %copy-start.1 = (f32[512,512]{1,0:T(8,128)S(1)}, f32[512,512]{1,0:T(8,128)}, u32[]{:S(2)}) copy-start(f32[512,512]{1,0:T(8,128)} %param.41) | copy-start | bytes 3145732
  219.6 142.7 %copy-start.23 = (f32[47,47]{1,0:T(8,128)S(1)}, f32[47,47]{1,0:T(8,128)}, u32[]{:S(2)}) copy-start(f32[47,47]{1,0:T(8,128)} %param.42) | copy-start | bytes 26512
  230.6 137.0 %copy-start.9 = (f32[256,256]{1,0:T(8,128)S(1)}, f32[256,256]{1,0:T(8,128)}, u32[]{:S(2)}) copy-start(f32[256,256]{1,0:T(8,128)} %param.40) | copy-start | bytes 786436
  232.3 135.3 %copy-start.12 = (f32[512,256]{1,0:T(8,128)S(1)}, f32[512,256]{1,0:T(8,128)}, u32[]{:S(2)}) copy-start(f32[512,256]{1,0:T(8,128)} %param.44) | copy-start | bytes 1572868
  360.5 7.2 %copy-start.13 = (f32[512,256]{1,0:T(8,128)S(1)}, f32[512,256]{1,0:T(8,128)}, u32[]{:S(2)}) copy-start(f32[512,256]{1,0:T(8,128)} %param.47) | copy-start | bytes 1572868
  363.5 7.4 %copy-start.15 = (f32[512,47]{0,1:T(8,128)}, f32[512,47]{0,1:T(8,128)S(1)}, u32[]{:S(2)}) copy-start(f32[512,47]{0,1:T(8,128)S(1)} %get-tuple-element.78) | copy-start | bytes 288772
  363.5 7.4 %copy-start.16 = (f32[512,47]{0,1:T(8,128)}, f32[512,47]{0,1:T(8,128)S(1)}, u32[]{:S(2)}) copy-start(f32[512,47]{0,1:T(8,128)S(1)} %get-tuple-element.79) | copy-start | bytes 288772
  367.7 5.0 %copy-start.21 = (f32[200,200]{1,0:T(8,128)S(1)}, f32[200,200]{1,0:T(8,128)}, u32[]{:S(2)}) copy-start(f32[200,200]{1,0:T(8,128)} %param.37) | copy-start | bytes 480004
  367.7 5.0 %copy-start.22 = (f32[200,256]{1,0:T(8,128)S(1)}, f32[200,256]{1,0:T(8,128)}, u32[]{:S(2)}) copy-start(f32[200,256]{1,0:T(8,128)} %get-tuple-element.58) | copy-start | bytes 614404
  367.7 5.6 %copy-start.7 = (f32[256,256]{1,0:T(8,128)S(1)}, f32[256,256]{1,0:T(8,128)}, u32[]{:S(2)}) copy-start(f32[256,256]{1,0:T(8,128)} %param.38) | copy-start | bytes 786436
  367.7 5.6 %copy-start.17 = (f32[200,256]{1,0:T(8,128)S(1)}, f32[200,256]{1,0:T(8,128)}, u32[]{:S(2)}) copy-start(f32[200,256]{1,0:T(8,128)} %param.43) | copy-start | bytes 614404
  367.7 5.6 %copy-start.18 = (f32[200,256]{1,0:T(8,128)S(1)}, f32[200,256]{1,0:T(8,128)}, u32[]{:S(2)}) copy-start(f32[200,256]{1,0:T(8,128)} %param.46) | copy-start | bytes 614404
  368.8 6.5 %copy-start.3 = (f32[512,256]{1,0:T(8,128)}, f32[512,256]{1,0:T(8,128)S(1)}, u32[]{:S(2)}) copy-start(f32[512,256]{1,0:T(8,128)S(1)} %get-tuple-element.64) | copy-start | bytes 1572868
  368.8 6.5 %copy-start.4 = (f32[512,256]{1,0:T(8,128)}, f32[512,256]{1,0:T(8,128)S(1)}, u32[]{:S(2)}) copy-start(f32[512,256]{1,0:T(8,128)S(1)} %get-tuple-element.65) | copy-start | bytes 1572868
  368.8 5.4 %copy-start.10 = (f32[200,256]{1,0:T(8,128)S(1)}, f32[200,256]{1,0:T(8,128)}, u32[]{:S(2)}) copy-start(f32[200,256]{1,0:T(8,128)} %param.34) | copy-start | bytes 614404
  373.7 1.6 copy-start.19
  373.7 1.6 copy-start.20
Sparse Core Ops, SparseCore 0:
  232.5 127.9 all-reduce.5
